TPU v7x, 32 devices: a whole 2x2x4 slice. The times are simulated.
32 devices in a mesh: depth: 8 (over z, y), chan: 4 (over x, core).
Axes of the slice: x: 2, y: 2, z: 4, core: 2. Of those that a mesh axis runs over, the one named last changes fastest.
Arguments:
- volume: bfloat16 [256, 8, 4096], P('chan', 'depth'), may hold values from -6 to 6
- w_first: bfloat16 [27, 256, 256], P(None, 'chan'), may hold values from -0.078125 to 0.078125
- b_first: float32 [256], P('chan'), may hold values from -3 to 3
- w_second: bfloat16 [27, 256, 256], P(None, None, 'chan'), may hold values from -0.078125 to 0.078125
- b_second: float32 [256], P('chan'), may hold values from -3 to 3
Outputs:
- block_out: bfloat16 [256, 8, 4096], P('chan', 'depth')
All inputs are finite; a program needn't handle non-finite values.
Results may differ from a plain program's by a relative error of at most 0.0043.
Values may be sent and summed in bfloat16 or wider, within the bound.
A program may use at most 128 MiB of HBM per device.

v0:
```python
import functools

import jax
import jax.numpy as jnp
from jax import lax
from jax.experimental import pallas as pl
from jax.experimental.pallas import tpu as pltpu
from jax.sharding import PartitionSpec as P

W = 64
PAD = 128
CHUNKS = 4
MESH = pl.DeviceIdType.MESH


def kernel(nd, nc, vol, w1, b1, w2, b2, out,
           xlo, xmid, xhi, w1t, w2t, cols1, cols2, s1s, s1r, keep, s2s, s2r,
           hpad, ps, pr, keep2,
           hal_s, hal_r, s1_ss, s1_rs, s2_ss, s2_rs, ag_ss, ag_rs, par_s, par_r):
    chan, cells = vol.shape
    total = chan * nc
    half = nc // 2
    size = cells // CHUNKS
    d = lax.axis_index("depth")
    c = lax.axis_index("chan")
    core = lax.rem(c, 2)
    chip = c // 2
    sibling = 2 * chip + 1 - core
    has_up = d < nd - 1
    has_down = d > 0

    def peer(k):
        return 2 * lax.rem(chip + k, half) + core

    zero_edge = jnp.zeros((chan, PAD), jnp.bfloat16)
    for pad in (xlo, xmid, xhi):
        pad[:, 0:PAD] = zero_edge
        pad[:, PAD + cells:] = zero_edge
    hpad[:, 0:PAD] = jnp.zeros((total, PAD), jnp.bfloat16)
    hpad[:, PAD + cells:] = jnp.zeros((total, PAD), jnp.bfloat16)

    @pl.when(d == 0)
    def _():
        xlo[:, PAD:PAD + cells] = jnp.zeros((chan, cells), jnp.bfloat16)
        pr[0] = jnp.zeros((chan, cells), jnp.bfloat16)

    @pl.when(d == nd - 1)
    def _():
        xhi[:, PAD:PAD + cells] = jnp.zeros((chan, cells), jnp.bfloat16)
        pr[1] = jnp.zeros((chan, cells), jnp.bfloat16)

    barrier = pltpu.get_barrier_semaphore()

    @pl.when(has_up)
    def _():
        pl.semaphore_signal(barrier, inc=1, device_id={"depth": d + 1}, device_id_type=MESH)

    @pl.when(has_down)
    def _():
        pl.semaphore_signal(barrier, inc=1, device_id={"depth": d - 1}, device_id_type=MESH)

    pl.semaphore_signal(barrier, inc=1, device_id={"chan": sibling}, device_id_type=MESH)
    for k in range(1, half):
        pl.semaphore_signal(barrier, inc=1, device_id={"chan": peer(k)}, device_id_type=MESH)

    pl.semaphore_wait(barrier, half + has_up.astype(jnp.int32) + has_down.astype(jnp.int32))

    def remote(src, dst, send, recv, where):
        return pltpu.make_async_remote_copy(
            src_ref=src, dst_ref=dst, send_sem=send, recv_sem=recv,
            device_id=where, device_id_type=MESH)

    def halo_up(n):
        return remote(vol.at[:, pl.ds(n * size, size)], xlo.at[:, pl.ds(PAD + n * size, size)],
                      hal_s.at[0, n], hal_r.at[0, n], {"depth": d + 1})

    def halo_down(n):
        return remote(vol.at[:, pl.ds(n * size, size)], xhi.at[:, pl.ds(PAD + n * size, size)],
                      hal_s.at[1, n], hal_r.at[1, n], {"depth": d - 1})

    for n in range(CHUNKS):
        @pl.when(has_up)
        def _():
            halo_up(n).start()

        @pl.when(has_down)
        def _():
            halo_down(n).start()

    xmid[:, PAD:PAD + cells] = vol[...]
    taps = 27 * chan
    for begin in range(0, taps, 128):
        end = min(begin + 128, taps)
        w1t[:, begin:end] = w1[begin:end, :].T
    for kd in range(3):
        for kk in range(9):
            w2t[kd * chan:(kd + 1) * chan, kk * total:(kk + 1) * total] = w2[kd * 9 + kk].T

    column = lax.broadcasted_iota(jnp.int32, (1, size), 1) % W
    left = jnp.where(column >= 1, 1.0, 0.0).astype(jnp.bfloat16)
    right = jnp.where(column < W - 1, 1.0, 0.0).astype(jnp.bfloat16)

    def nine(pad, n, dst, row):
        rows = pad.shape[0]
        for kh in range(3):
            for kw in range(3):
                begin = PAD + n * size + (kh - 1) * W + kw - 1
                value = pad[:, begin:begin + size]
                if kw == 0:
                    value = value * left
                elif kw == 2:
                    value = value * right
                dst[row:row + rows, :] = value
                row += rows

    def halo_wait(n):
        @pl.when(has_down)
        def _():
            halo_up(n).wait_recv()

        @pl.when(has_up)
        def _():
            halo_down(n).wait_recv()

    def step1(n):
        return remote(s1s.at[n], s1r.at[n], s1_ss.at[n], s1_rs.at[n], {"chan": sibling})

    def first(n):
        if n == 0:
            halo_wait(0)
        if n + 1 < CHUNKS:
            halo_wait(n + 1)
        for kd, pad in enumerate((xlo, xmid, xhi)):
            nine(pad, n, cols1, kd * 9 * chan)
        acc = jnp.dot(w1t[...], cols1[...], preferred_element_type=jnp.float32)
        for j in range(half):
            even = acc[2 * j * chan:(2 * j + 1) * chan]
            odd = acc[(2 * j + 1) * chan:(2 * j + 2) * chan]
            rows = slice(j * chan, (j + 1) * chan)
            keep[n, rows, :] = jnp.where(core == 0, even, odd)
            s1s[n, rows, :] = jnp.where(core == 0, odd, even).astype(jnp.bfloat16)
        step1(n).start()

    def step2(n, k):
        block = pl.ds(pl.multiple_of(lax.rem(chip + k, half) * chan, chan), chan)
        return remote(s2s.at[n, block], s2r.at[n, k - 1], s2_ss.at[n, k - 1], s2_rs.at[n, k - 1],
                      {"chan": peer(k)})

    def second(n):
        step1(n).wait_recv()
        both = keep[n] + s1r[n].astype(jnp.float32)
        keep[n] = both
        s2s[n] = both.astype(jnp.bfloat16)
        for k in range(1, half):
            step2(n, k).start()

    def block_of(owner, n):
        return hpad.at[pl.ds(pl.multiple_of(owner * chan, chan), chan), pl.ds(PAD + n * size, size)]

    def gather_peer(n, k):
        here = block_of(c, n)
        return remote(here, here, ag_ss.at[n, k], ag_rs.at[n, k], {"chan": peer(k)})

    def gather_sibling(n, k):
        here = block_of(peer(half - k), n)
        return remote(here, here, ag_ss.at[n, half + k], ag_rs.at[n, half + k], {"chan": sibling})

    def third(n):
        total_sum = keep[n, pl.ds(pl.multiple_of(chip * chan, chan), chan), :]
        for k in range(1, half):
            step2(n, k).wait_recv()
            total_sum = total_sum + s2r[n, k - 1].astype(jnp.float32)
        hidden = jnp.maximum(total_sum + b1[...], 0.0).astype(jnp.bfloat16)
        hpad[pl.ds(pl.multiple_of(c * chan, chan), chan), PAD + n * size:PAD + (n + 1) * size] = hidden
        for k in range(1, half):
            gather_peer(n, k).start()
        gather_sibling(n, 0).start()

    def forward(n):
        for k in range(1, half):
            gather_peer(n, k).wait_recv()
            gather_sibling(n, k).start()

    def gathered(n):
        for k in range(half):
            gather_sibling(n, k).wait_recv()

    def partial_up(n):
        columns = pl.ds(n * size, size)
        return remote(ps.at[0, :, columns], pr.at[0, :, columns], par_s.at[0, n], par_r.at[0, n],
                      {"depth": d + 1})

    def partial_down(n):
        columns = pl.ds(n * size, size)
        return remote(ps.at[1, :, columns], pr.at[1, :, columns], par_s.at[1, n], par_r.at[1, n],
                      {"depth": d - 1})

    def fourth(n):
        nine(hpad, n, cols2, 0)
        acc = jnp.dot(w2t[...], cols2[...], preferred_element_type=jnp.float32)
        columns = slice(n * size, (n + 1) * size)
        ps[0, :, columns] = acc[0:chan].astype(jnp.bfloat16)
        ps[1, :, columns] = acc[2 * chan:3 * chan].astype(jnp.bfloat16)

        @pl.when(has_up)
        def _():
            partial_up(n).start()

        @pl.when(has_down)
        def _():
            partial_down(n).start()

        keep2[:, columns] = acc[chan:2 * chan] + b2[...]

    def last(n):
        @pl.when(has_down)
        def _():
            partial_up(n).wait_recv()

        @pl.when(has_up)
        def _():
            partial_down(n).wait_recv()

        columns = slice(n * size, (n + 1) * size)
        value = keep2[:, columns] + pr[0, :, columns].astype(jnp.float32)
        out[:, columns] = (value + pr[1, :, columns].astype(jnp.float32)).astype(jnp.bfloat16)

    for t in range(CHUNKS + 4):
        if t < CHUNKS:
            first(t)
            second(t)
        if 0 <= t - 1 < CHUNKS:
            third(t - 1)
            forward(t - 1)
        if 0 <= t - 2 < CHUNKS:
            gathered(t - 2)
        if 0 <= t - 3 < CHUNKS:
            fourth(t - 3)
    for n in range(CHUNKS):
        last(n)

    for n in range(CHUNKS):
        @pl.when(has_up)
        def _():
            halo_up(n).wait_send()
            partial_up(n).wait_send()

        @pl.when(has_down)
        def _():
            halo_down(n).wait_send()
            partial_down(n).wait_send()

        step1(n).wait_send()
        gather_sibling(n, 0).wait_send()
        for k in range(1, half):
            step2(n, k).wait_send()
            gather_peer(n, k).wait_send()
            gather_sibling(n, k).wait_send()


def body(nd, nc, volume, w_first, b_first, w_second, b_second):
    chan, slab, cells = volume.shape
    total, half, size = chan * nc, nc // 2, cells // CHUNKS
    bf16, f32 = jnp.bfloat16, jnp.float32
    vmem = pl.BlockSpec(memory_space=pltpu.VMEM)
    dma = pltpu.SemaphoreType.DMA
    wide = cells + 2 * PAD
    out = pl.pallas_call(
        functools.partial(kernel, nd, nc),
        out_shape=jax.ShapeDtypeStruct((chan, cells), bf16),
        in_specs=[vmem] * 5,
        out_specs=vmem,
        scratch_shapes=[
            pltpu.VMEM((chan, wide), bf16),
            pltpu.VMEM((chan, wide), bf16),
            pltpu.VMEM((chan, wide), bf16),
            pltpu.VMEM((total, 27 * chan), bf16),
            pltpu.VMEM((3 * chan, 9 * total), bf16),
            pltpu.VMEM((27 * chan, size), bf16),
            pltpu.VMEM((9 * total, size), bf16),
            pltpu.VMEM((CHUNKS, half * chan, size), bf16),
            pltpu.VMEM((CHUNKS, half * chan, size), bf16),
            pltpu.VMEM((CHUNKS, half * chan, size), f32),
            pltpu.VMEM((CHUNKS, half * chan, size), bf16),
            pltpu.VMEM((CHUNKS, half - 1, chan, size), bf16),
            pltpu.VMEM((total, wide), bf16),
            pltpu.VMEM((2, chan, cells), bf16),
            pltpu.VMEM((2, chan, cells), bf16),
            pltpu.VMEM((chan, cells), f32),
            dma((2, CHUNKS)), dma((2, CHUNKS)),
            dma((CHUNKS,)), dma((CHUNKS,)),
            dma((CHUNKS, half - 1)), dma((CHUNKS, half - 1)),
            dma((CHUNKS, 2 * half)), dma((CHUNKS, 2 * half)),
            dma((2, CHUNKS)), dma((2, CHUNKS)),
        ],
        compiler_params=pltpu.CompilerParams(
            collective_id=0, has_side_effects=True, vmem_limit_bytes=56 * 1024 * 1024),
    )(
        volume.reshape(chan, cells),
        w_first.reshape(27 * chan, total),
        b_first.reshape(chan, 1),
        w_second,
        b_second.reshape(chan, 1),
    )
    return out.reshape(chan, slab, cells)


def solution(mesh):
    in_specs = (
        P("chan", "depth", None),
        P(None, "chan", None),
        P("chan"),
        P(None, None, "chan"),
        P("chan"),
    )
    out_specs = P("chan", "depth", None)
    inner = functools.partial(body, mesh.shape["depth"], mesh.shape["chan"])
    return jax.shard_map(inner, mesh=mesh, in_specs=in_specs, out_specs=out_specs, check_vma=False)
```

profile of v0, /device:TPU:20, one launch (start us, length us, event | category | flops | bytes accessed | tf_op | source)
XLA Modules:
  0.0 91.2 jit_solution(3561518396153680884)
XLA Ops:
  0.0 1.4 %copy.6.b1 = f32[64,1]{1,0:T(8,128)} copy(f32[64,1]{0,1:T(1,128)} %bitcast.8) | data formatting | bytes 512 | tf_op jit(solution)/shard_map/reshape | solution.py:301
  1.4 1.3 %copy.8.b2 = f32[64,1]{1,0:T(8,128)} copy(f32[64,1]{0,1:T(1,128)} %bitcast.9) | data formatting | bytes 512 | tf_op jit(solution)/shard_map/reshape | solution.py:303
  2.7 2.6 %copy.7.w2 = bf16[27,256,64]{2,1,0:T(8,128)(2,1)} copy(bf16[27,256,64]{1,2,0:T(8,128)(2,1)} %param.8) | data formatting | bytes 1769472 | tf_op args[3]
  5.3 84.1 %shard_map.55 = bf16[64,4096]{1,0:T(8,128)(2,1)} custom-call(bf16[64,4096]{1,0:T(8,128)(2,1)} %bitcast.7, bf16[1728,256]{1,0:T(8,128)(2,1)} %bitcast.6, f32[64,1]{1,0:T(8,128)} %copy.6.b1, bf16[27,256,64]{2,1,0:T(8,128)(2,1)} %copy.7.w2, f32[64,1]{1,0:T(8,128)} %copy.8.b2), custom_call_target="tpu_custom_call" | custom-call | tf_op jit(solution)/shard_map/pallas_call | solution.py:268
  89.4 1.9 %copy.10 = bf16[64,1,4096]{2,0,1:T(8,128)(2,1)} copy(bf16[64,1,4096]{2,0,1:T(8,128)(2,1)} %bitcast.5) | data formatting | bytes 1048576
where the time goes:
time: 92.1 us; the launch traced here: 91.2 us
  Pallas kernels  84.1 us (91%)
  local copies, waits for them, and re-layouts  7.14 us (8%)
    pallas_call x1, Pallas kernels, body(): pl.pallas_call(functools.partial(kernel, nd, nc), out_shape=jax.ShapeDtyp...  84.1 us
    unnamed x2, local copies, waits for them, and re-layouts  4.44 us

commit v1 on v0

v1 whole, which is shorter than its diff:
```python
import functools

import jax
import jax.numpy as jnp
from jax import lax
from jax.experimental import pallas as pl
from jax.experimental.pallas import tpu as pltpu
from jax.sharding import PartitionSpec as P

W = 64
PAD = 128
MESH = pl.DeviceIdType.MESH


def kernel(nd, nc, vol, w1, b1, w2, b2, out,
           xs, w1t, w2t, cols1, cols2, s1s, s1r, keep, s2s, s2r,
           hpad, ps, pr, total_a, total_b, done, landed,
           pair_s, pair_r, z_s, z_r, s1_ss, s1_rs, s2_ss, s2_rs, ag_ss, ag_rs, par_s, par_r):
    chan, cells = vol.shape
    total = chan * nc
    half = nc // 2
    inner = cells // 2
    seg = inner + PAD
    skip = inner - PAD
    spans, spans2, pieces = chunk_spans(cells)
    count = len(spans)
    d = lax.axis_index("depth")
    c = lax.axis_index("chan")
    side = lax.rem(d, 2)
    partner = d + 1 - 2 * side
    core = lax.rem(c, 2)
    chip = c // 2
    sibling = 2 * chip + 1 - core
    has_up = d + 2 < nd
    has_down = d >= 2

    def peer(k):
        return 2 * lax.rem(chip + k, half) + core

    for plane in range(4):
        xs[plane, :, 0:PAD] = jnp.zeros((chan, PAD), jnp.bfloat16)
        xs[plane, :, PAD + seg:] = jnp.zeros((chan, PAD), jnp.bfloat16)
    for plane in range(2):
        hpad[plane, :, 0:PAD] = jnp.zeros((total, PAD), jnp.bfloat16)
        hpad[plane, :, PAD + seg:] = jnp.zeros((total, PAD), jnp.bfloat16)

    @pl.when(jnp.logical_not(has_down))
    def _():
        xs[0, :, PAD:PAD + seg] = jnp.zeros((chan, seg), jnp.bfloat16)
        pr[0] = jnp.zeros((chan, seg), jnp.bfloat16)

    @pl.when(jnp.logical_not(has_up))
    def _():
        xs[3, :, PAD:PAD + seg] = jnp.zeros((chan, seg), jnp.bfloat16)
        pr[1] = jnp.zeros((chan, seg), jnp.bfloat16)

    barrier = pltpu.get_barrier_semaphore()

    @pl.when(has_up)
    def _():
        pl.semaphore_signal(barrier, inc=1, device_id={"depth": d + 2}, device_id_type=MESH)

    @pl.when(has_down)
    def _():
        pl.semaphore_signal(barrier, inc=1, device_id={"depth": d - 2}, device_id_type=MESH)

    pl.semaphore_signal(barrier, inc=1, device_id={"depth": partner}, device_id_type=MESH)
    pl.semaphore_signal(barrier, inc=1, device_id={"chan": sibling}, device_id_type=MESH)
    for k in range(1, half):
        pl.semaphore_signal(barrier, inc=1, device_id={"chan": peer(k)}, device_id_type=MESH)
    pl.semaphore_wait(barrier, half + 1 + has_up.astype(jnp.int32) + has_down.astype(jnp.int32))

    def remote(src, dst, send, recv, where):
        return pltpu.make_async_remote_copy(
            src_ref=src, dst_ref=dst, send_sem=send, recv_sem=recv,
            device_id=where, device_id_type=MESH)

    def swap(i):
        start, size = pieces[i]
        theirs = pl.ds(pl.multiple_of((1 - side) * skip + start, PAD), size)
        return remote(vol.at[:, theirs], xs.at[1 + side, :, pl.ds(PAD + start, size)],
                      pair_s.at[i], pair_r.at[i], {"depth": partner})

    def send_up(i):
        data = pl.ds(PAD + pieces[i][0], pieces[i][1])
        return remote(xs.at[2, :, data], xs.at[0, :, data], z_s.at[0, i], z_r.at[0, i], {"depth": d + 2})

    def send_down(i):
        data = pl.ds(PAD + pieces[i][0], pieces[i][1])
        return remote(xs.at[1, :, data], xs.at[3, :, data], z_s.at[1, i], z_r.at[1, i], {"depth": d - 2})

    def own_out(i):
        @pl.when(jnp.logical_and(side == 0, has_down))
        def _():
            send_down(i).start()

        @pl.when(jnp.logical_and(side == 1, has_up))
        def _():
            send_up(i).start()

    def relay(i):
        swap(i).wait_recv()

        @pl.when(jnp.logical_and(side == 1, has_down))
        def _():
            send_down(i).start()

        @pl.when(jnp.logical_and(side == 0, has_up))
        def _():
            send_up(i).start()

    swap(0).start()
    xs[1 + side, :, PAD:PAD + seg] = vol[:, pl.ds(pl.multiple_of(side * skip, PAD), seg)]
    own_out(0)
    bias1 = jnp.broadcast_to(b1[...], (8, chan)).T[:, 0:1]
    bias2 = jnp.broadcast_to(b2[...], (8, chan)).T[:, 0:1]
    taps = 27 * chan
    for begin in range(0, taps, 128):
        end = min(begin + 128, taps)
        w1t[:, begin:end] = w1[begin:end, :].T
    relay(0)
    swap(1).start()
    own_out(1)
    for kd in range(3):
        for kk in range(9):
            w2t[kd * chan:(kd + 1) * chan, kk * total:(kk + 1) * total] = w2[kd * 9 + kk]

    def nine(pad, plane, start, size, dst, row):
        rows = pad.shape[1]
        column = lax.broadcasted_iota(jnp.int32, (1, size), 1) % W
        left = jnp.where(column >= 1, 1.0, 0.0).astype(jnp.bfloat16)
        right = jnp.where(column < W - 1, 1.0, 0.0).astype(jnp.bfloat16)
        for kh in range(3):
            for kw in range(3):
                begin = PAD + start + (kh - 1) * W + kw - 1
                value = pad[plane, :, begin:begin + size]
                if kw == 0:
                    value = value * left
                elif kw == 2:
                    value = value * right
                dst[row:row + rows, 0:size] = value
                row += rows

    def step1(n):
        size = spans[n][2]
        return remote(s1s.at[n, :, pl.ds(0, size)], s1r.at[n, :, pl.ds(0, size)],
                      s1_ss.at[n], s1_rs.at[n], {"chan": sibling})

    def first(n):
        plane, start, size = spans[n]
        for kd in range(3):
            nine(xs, plane + kd, start, size, cols1, kd * 9 * chan)
        acc = jnp.dot(w1t[...], cols1[:, 0:size], preferred_element_type=jnp.float32)
        for j in range(half):
            even = acc[2 * j * chan:(2 * j + 1) * chan]
            odd = acc[(2 * j + 1) * chan:(2 * j + 2) * chan]
            rows = slice(j * chan, (j + 1) * chan)
            keep[n, rows, 0:size] = jnp.where(core == 0, even, odd)
            s1s[n, rows, 0:size] = jnp.where(core == 0, odd, even).astype(jnp.bfloat16)
        step1(n).start()

    def step2(n, k):
        size = spans[n][2]
        block = pl.ds(pl.multiple_of(lax.rem(chip + k, half) * chan, chan), chan)
        return remote(s2s.at[n, block, pl.ds(0, size)], s2r.at[n, k - 1, :, pl.ds(0, size)],
                      s2_ss.at[n, k - 1], s2_rs.at[n, k - 1], {"chan": peer(k)})

    def second(n):
        size = spans[n][2]
        step1(n).wait_recv()
        both = keep[n, :, 0:size] + s1r[n, :, 0:size].astype(jnp.float32)
        keep[n, :, 0:size] = both
        s2s[n, :, 0:size] = both.astype(jnp.bfloat16)
        for k in range(1, half):
            step2(n, k).start()

    def block_of(owner, n):
        plane, start, size = spans[n]
        return hpad.at[plane, pl.ds(pl.multiple_of(owner * chan, chan), chan), pl.ds(PAD + start, size)]

    def gather_peer(n, k):
        here = block_of(c, n)
        return remote(here, here, ag_ss.at[n, k], ag_rs.at[n, k], {"chan": peer(k)})

    def gather_sibling(n, k):
        here = block_of(peer(half - k), n)
        return remote(here, here, ag_ss.at[n, half + k], ag_rs.at[n, half + k], {"chan": sibling})

    def third(n):
        plane, start, size = spans[n]
        value = keep[n, pl.ds(pl.multiple_of(chip * chan, chan), chan), 0:size]
        for k in range(1, half):
            step2(n, k).wait_recv()
            value = value + s2r[n, k - 1, :, 0:size].astype(jnp.float32)
        hidden = jnp.maximum(value + bias1, 0.0).astype(jnp.bfloat16)
        hpad[plane, pl.ds(pl.multiple_of(c * chan, chan), chan), PAD + start:PAD + start + size] = hidden
        for k in range(1, half):
            gather_peer(n, k).start()
        gather_sibling(n, 0).start()

    def forward(n):
        for k in range(1, half):
            gather_peer(n, k).wait_recv()
            gather_sibling(n, k).start()

    def gathered(n):
        for k in range(half):
            gather_sibling(n, k).wait_recv()

    def partial(n):
        plane, start, size = spans2[n]
        columns = pl.ds(start, size)
        index = 1 - plane
        return remote(ps.at[index, :, columns], pr.at[index, :, columns],
                      par_s.at[n], par_r.at[n], {"depth": d + 4 * plane - 2})

    def fourth(n):
        plane, start, size = spans2[n]
        nine(hpad, plane, start, size, cols2, 0)
        acc = jnp.dot(w2t[...], cols2[:, 0:size], preferred_element_type=jnp.float32)
        columns = slice(start, start + size)
        below, same, above = acc[0:chan], acc[chan:2 * chan], acc[2 * chan:3 * chan]
        if plane == 0:
            ps[1, :, columns] = above.astype(jnp.bfloat16)
            total_a[:, columns] = same + bias2
            total_b[:, columns] = below + bias2
        else:
            ps[0, :, columns] = below.astype(jnp.bfloat16)
            total_a[:, columns] = total_a[:, columns] + above
            total_b[:, columns] = total_b[:, columns] + same

        @pl.when(has_up if plane else has_down)
        def _():
            partial(n).start()

    def last(n):
        plane, start, size = spans2[n]

        @pl.when(has_down if plane else has_up)
        def _():
            partial(n).wait_recv()

        columns = slice(start, start + size)
        index = 1 - plane
        held = total_b if index else total_a
        value = held[:, columns] + pr[index, :, columns].astype(jnp.float32)
        done[index, :, columns] = value.astype(jnp.bfloat16)

    def arrived(t):
        @pl.when(has_up if t % 2 else has_down)
        def _():
            (send_down if t % 2 else send_up)(t // 2).wait_recv()

    tail = inner // 2 + PAD
    parts = [(0, inner - tail), (inner - tail, tail)]

    def back(i):
        start, size = parts[i]
        return remote(done.at[1 - side, :, pl.ds(pl.multiple_of(side * PAD + start, PAD), size)],
                      landed.at[:, pl.ds(start, size)], pair_s.at[2 + i], pair_r.at[2 + i],
                      {"depth": partner})

    def finish(i):
        last(2 * i)
        last(2 * i + 1)
        back(i).start()

    for t in range(count + 2):
        if t < count:
            arrived(t)
            first(t)
            if t == 0:
                relay(1)
        if 0 <= t - 1 < count:
            third(t - 1)
        if t < count:
            second(t)
        if 0 <= t - 2 < count:
            gathered(t - 2)
            fourth(t - 2)
        if 0 <= t - 1 < count:
            forward(t - 1)
        if t == count:
            finish(0)
    finish(1)

    out[:, pl.ds(pl.multiple_of(side * inner, PAD), inner)] = done[
        side, :, pl.ds(pl.multiple_of(side * PAD, PAD), inner)]
    for i, (start, size) in enumerate(parts):
        back(i).wait_recv()
        out[:, pl.ds(pl.multiple_of((1 - side) * inner + start, PAD), size)] = landed[:, start:start + size]

    for i in range(2):
        back(i).wait_send()
        swap(i).wait_send()

        @pl.when(has_up)
        def _():
            send_up(i).wait_send()

        @pl.when(has_down)
        def _():
            send_down(i).wait_send()

    for n in range(count):
        @pl.when(has_up if spans[n][0] else has_down)
        def _():
            partial(n).wait_send()

        step1(n).wait_send()
        gather_sibling(n, 0).wait_send()
        for k in range(1, half):
            step2(n, k).wait_send()
            gather_peer(n, k).wait_send()
            gather_sibling(n, k).wait_send()


def chunk_spans(cells):
    seg = cells // 2 + PAD
    cut = (seg // 2 + PAD - 1) // PAD * PAD
    early = cut - PAD
    first = [(plane, start, size) for start, size in ((0, cut), (cut, seg - cut)) for plane in range(2)]
    second = [(plane, start, size) for start, size in ((0, early), (early, seg - early)) for plane in range(2)]
    pieces = [(0, cut + PAD), (cut + PAD, seg - cut - PAD)]
    return first, second, pieces


def body(nd, nc, volume, w_first, b_first, w_second, b_second):
    chan, slab, cells = volume.shape
    total, half = chan * nc, nc // 2
    spans, spans2, pieces = chunk_spans(cells)
    count = len(spans)
    size = max(span[2] for span in spans + spans2)
    seg = cells // 2 + PAD
    bf16, f32 = jnp.bfloat16, jnp.float32
    vmem = pl.BlockSpec(memory_space=pltpu.VMEM)
    dma = pltpu.SemaphoreType.DMA
    wide = seg + 2 * PAD
    out = pl.pallas_call(
        functools.partial(kernel, nd, nc),
        out_shape=jax.ShapeDtypeStruct((chan, cells), bf16),
        in_specs=[vmem] * 5,
        out_specs=vmem,
        scratch_shapes=[
            pltpu.VMEM((4, chan, wide), bf16),
            pltpu.VMEM((total, 27 * chan), bf16),
            pltpu.VMEM((3 * chan, 9 * total), bf16),
            pltpu.VMEM((27 * chan, size), bf16),
            pltpu.VMEM((9 * total, size), bf16),
            pltpu.VMEM((count, half * chan, size), bf16),
            pltpu.VMEM((count, half * chan, size), bf16),
            pltpu.VMEM((count, half * chan, size), f32),
            pltpu.VMEM((count, half * chan, size), bf16),
            pltpu.VMEM((count, half - 1, chan, size), bf16),
            pltpu.VMEM((2, total, wide), bf16),
            pltpu.VMEM((2, chan, seg), bf16),
            pltpu.VMEM((2, chan, seg), bf16),
            pltpu.VMEM((chan, seg), f32),
            pltpu.VMEM((chan, seg), f32),
            pltpu.VMEM((2, chan, seg), bf16),
            pltpu.VMEM((chan, cells // 2), bf16),
            dma((4,)), dma((4,)), dma((2, 2)), dma((2, 2)),
            dma((count,)), dma((count,)),
            dma((count, half - 1)), dma((count, half - 1)),
            dma((count, 2 * half)), dma((count, 2 * half)),
            dma((count,)), dma((count,)),
        ],
        compiler_params=pltpu.CompilerParams(
            collective_id=0, has_side_effects=True, vmem_limit_bytes=56 * 1024 * 1024),
    )(
        volume.reshape(chan, cells),
        w_first.reshape(27 * chan, total),
        b_first.reshape(1, chan),
        jnp.swapaxes(w_second, 1, 2),
        b_second.reshape(1, chan),
    )
    return out.reshape(chan, slab, cells)


def solution(mesh):
    in_specs = (
        P("chan", "depth", None),
        P(None, "chan", None),
        P("chan"),
        P(None, None, "chan"),
        P("chan"),
    )
    out_specs = P("chan", "depth", None)
    inner = functools.partial(body, mesh.shape["depth"], mesh.shape["chan"])
    return jax.shard_map(inner, mesh=mesh, in_specs=in_specs, out_specs=out_specs, check_vma=False)
```

time: 92.1 us -> 64.3 us (0.70)
  Pallas kernels: 84.1 us -> 62.2 us
  local copies, waits for them, and re-layouts: 7.14 us -> 1.87 us
    pallas_call x1, Pallas kernels: 84.1 us -> 62.2 us  [body(): pl.pallas_call(functools.partial(kernel, nd, nc), out_shape=jax.ShapeDtyp...]
    reshape x2 -> x0, local copies, waits for them, and re-layouts: 2.7 us -> none  [the longest x1 1.36 us: body(): b_first.reshape(chan, 1)]
    unnamed x2 -> x1, local copies, waits for them, and re-layouts: 4.44 us -> 1.87 us
where the time goes in v1:
time: 64.3 us; the launch traced here: 64.1 us
  Pallas kernels  62.2 us (97%)
  local copies, waits for them, and re-layouts  1.87 us (3%)
    pallas_call x1, Pallas kernels, body(): pl.pallas_call(functools.partial(kernel, nd, nc), out_shape=jax.ShapeDtyp...  62.2 us
    unnamed x1, local copies, waits for them, and re-layouts  1.87 us

profile of v1, /device:TPU:20, one launch (start us, length us, event | category | flops | bytes accessed | tf_op | source)
XLA Modules:
  0.0 64.1 jit_solution(6658760548544498768)
XLA Ops:
  0.0 62.2 %shard_map.55 = bf16[64,4096]{1,0:T(8,128)(2,1)} custom-call(bf16[64,4096]{1,0:T(8,128)(2,1)} %bitcast.9, bf16[1728,256]{1,0:T(8,128)(2,1)} %bitcast.7, f32[1,64]{1,0:T(1,128)} %bitcast.10, bf16[27,64,256]{2,1,0:T(8,128)(2,1)} %bitcast.8, f32[1,64]{1,0:T(1,128)} %bitcast.11), custom_call_target="tpu_custom_call" | custom-call | tf_op jit(solution)/shard_map/pallas_call | solution.py:339
  62.2 1.9 %copy.7 = bf16[64,1,4096]{2,0,1:T(8,128)(2,1)} copy(bf16[64,1,4096]{2,0,1:T(8,128)(2,1)} %bitcast.6) | data formatting | bytes 1048576

commit v2 on v1

--- a/solution.py
+++ b/solution.py
@@ -273,11 +273,11 @@
                 relay(1)
         if 0 <= t - 1 < count:
             third(t - 1)
-        if t < count:
-            second(t)
         if 0 <= t - 2 < count:
             gathered(t - 2)
             fourth(t - 2)
+        if t < count:
+            second(t)
         if 0 <= t - 1 < count:
             forward(t - 1)
         if t == count:

time: 64.3 us -> 64.3 us (level)
  no operation moved by 1% of the time
where the time goes in v2:
time: 64.3 us; the launch traced here: 64.1 us
  Pallas kernels  62.2 us (97%)
  local copies, waits for them, and re-layouts  1.87 us (3%)
    pallas_call x1, Pallas kernels, body(): pl.pallas_call(functools.partial(kernel, nd, nc), out_shape=jax.ShapeDtyp...  62.2 us
    unnamed x1, local copies, waits for them, and re-layouts  1.87 us

profile of v2, /device:TPU:20, one launch (start us, length us, event | category | flops | bytes accessed | tf_op | source)
XLA Modules:
  0.0 64.1 jit_solution(10531493403435970617)
XLA Ops:
  0.0 62.2 %shard_map.55 = bf16[64,4096]{1,0:T(8,128)(2,1)} custom-call(bf16[64,4096]{1,0:T(8,128)(2,1)} %bitcast.9, bf16[1728,256]{1,0:T(8,128)(2,1)} %bitcast.7, f32[1,64]{1,0:T(1,128)} %bitcast.10, bf16[27,64,256]{2,1,0:T(8,128)(2,1)} %bitcast.8, f32[1,64]{1,0:T(1,128)} %bitcast.11), custom_call_target="tpu_custom_call" | custom-call | tf_op jit(solution)/shard_map/pallas_call | solution.py:339
  62.2 1.9 %copy.7 = bf16[64,1,4096]{2,0,1:T(8,128)(2,1)} copy(bf16[64,1,4096]{2,0,1:T(8,128)(2,1)} %bitcast.6) | data formatting | bytes 1048576
